TPU v7x, 256 devices: a whole 4x4x8 slice. The times are simulated.
256 devices in a mesh: tower: 2 (over core), depth: 32 (over y, z), sub: 4 (over x).
Axes of the slice: x: 4, y: 4, z: 8, core: 2. Of those that a mesh axis runs over, the one named last changes fastest.
Arguments:
- embeds: bfloat16 [2, 131072, 1024], P('tower', ('depth', 'sub')), may hold values from -700 to 700
- counts: int32 [128], P(('depth', 'sub')), may hold values from 256 to 1024, as said below
Outputs:
- row_grads: bfloat16 [2, 131072, 1024], P('tower', ('depth', 'sub'))
- corr_mean: float32 [], replicated
Inputs may be any that keep to these rules, and one draw needn't show every extreme that they name: `counts`: block b holds at least 256 and at most 256 + 768 * b // 127 valid samples; the first block holds exactly 256 and the last block is full.
All inputs are finite; a program needn't handle non-finite values.
Results may differ from a plain program's by a relative error of at most 0.022.
Values may be sent and summed in bfloat16 or wider, within the bound.
A program may use at most 128 MiB of HBM per device.

v0:
```python
import jax
import jax.numpy as jnp
from jax import lax
from jax.sharding import PartitionSpec as P

REG = 0.001
contract_rows = (((0,), (0,)), ((), ()))


def from_partner(value, axis, apart):
    mask = 2**apart
    pairs = [(source, source ^ mask) for source in range(lax.axis_size(axis))]
    return lax.ppermute(value, axis, pairs)


def whitening(block_rows, valid_rows, gram_total, column_sum, count_total):
    feature_width = block_rows.shape[1]
    column_mean = column_sum / count_total
    covariance = (gram_total - jnp.outer(column_sum, column_mean)) / (
        count_total - 1.0
    ) + REG * jnp.eye(feature_width, dtype=jnp.float32)
    factor_lower = jnp.linalg.cholesky(covariance)
    centered = jnp.where(
        valid_rows[:, None], block_rows.astype(jnp.float32) - column_mean[None, :], 0.0
    )
    whitened = jax.scipy.linalg.solve_triangular(factor_lower, centered.T, lower=True).T
    return (whitened.astype(jnp.bfloat16), factor_lower)


def gradient_rows(own_white, other_white, turned, factor_lower, valid_rows):
    product_rows = jnp.dot(own_white, turned, preferred_element_type=jnp.float32)
    residual = (other_white.astype(jnp.float32) - product_rows).astype(jnp.bfloat16)
    back_rows = lax.dot_general(
        residual, turned, (((1,), (1,)), ((), ())), preferred_element_type=jnp.float32
    )
    solved = jax.scipy.linalg.solve_triangular(factor_lower, back_rows.T, lower=True, trans=1).T
    return jnp.where(valid_rows[:, None], solved, 0.0).astype(jnp.bfloat16)


def on_device(embeds, counts):
    block_rows = embeds[0]
    rows_local = block_rows.shape[0]
    feature_width = block_rows.shape[1]
    valid_rows = lax.iota(jnp.int32, rows_local) < counts[0]
    log_tower = lax.axis_index("tower") == 0
    count_part = counts.astype(jnp.float32)
    masked = jnp.where(valid_rows[:, None], block_rows, jnp.zeros_like(block_rows))
    gram_part = lax.dot_general(masked, masked, contract_rows, preferred_element_type=jnp.float32)
    column_part = jnp.sum(masked, axis=0, dtype=jnp.float32)
    gram_total, column_sum, count_sums = lax.psum(
        (gram_part, column_part, count_part), ("depth", "sub")
    )
    count_total = count_sums[0]
    whitened, factor_lower = whitening(block_rows, valid_rows, gram_total, column_sum, count_total)
    partner_rows = from_partner(whitened, "tower", 0)
    log_white = jnp.where(log_tower, whitened, partner_rows)
    image_white = jnp.where(log_tower, partner_rows, whitened)
    half_rows = rows_local // 2
    first_row = lax.axis_index("tower") * half_rows
    log_part = lax.dynamic_slice_in_dim(log_white, first_row, half_rows, 0)
    image_part = lax.dynamic_slice_in_dim(image_white, first_row, half_rows, 0)
    group_size = lax.axis_size(("tower", "depth", "sub"))
    cross_part = lax.dot_general(
        log_part, image_part, contract_rows, preferred_element_type=jnp.float32
    )
    cross_share = lax.psum_scatter(
        cross_part.reshape(group_size, -1),
        ("tower", "depth", "sub"),
        scatter_dimension=0,
        tiled=True,
    )
    share_bf = (cross_share / (count_total - 1.0)).astype(jnp.bfloat16)
    gathered = lax.all_gather(share_bf, ("tower", "depth", "sub"), axis=0, tiled=True)
    cross_bf = gathered.reshape(feature_width, feature_width)
    corr_mean = jnp.sum(jnp.square(cross_bf.astype(jnp.float32))) / feature_width
    turned = jnp.where(log_tower, cross_bf, cross_bf.T)
    gradient = gradient_rows(whitened, partner_rows, turned, factor_lower, valid_rows)
    return (gradient[None], corr_mean)


def solution(mesh):
    placed = (P("tower", ("depth", "sub"), None), P(("depth", "sub")))
    return jax.shard_map(
        on_device,
        mesh=mesh,
        in_specs=placed,
        out_specs=(P("tower", ("depth", "sub"), None), P()),
        check_vma=False,
    )
```

profile of v0, /device:TPU:1, one launch (start us, length us, event | category | flops | bytes accessed | tf_op | source)
XLA Modules:
  0.0 1235.0 jit_solution(12310317839092781534)
XLA Ops:
  7.9 6.7 fusion.19
  18.0 303.9 %all-reduce.2 = (f32[1024]{0:T(1024)S(1)}, f32[]{:T(128)}) all-reduce(f32[1024]{0:T(1024)S(1)} %convert_reduce_fusion, f32[]{:T(128)} %bitcast.3), channel_id=1, replica_groups=mesh['tower'=2,'depth'=32,'sub'=4] {'depth','sub'}, use_global_device_ids=true, to_apply=%region_2.3 | all-reduce | flops 1025 | bytes 8200 | tf_op jit(solution)/shard_map/psum | solution.py:50
  323.3 5.7 select_add_fusion
  329.0 5.8 copy.62
  334.8 4.4 fusion
  341.2 11.7 cholesky.222
  353.0 9.8 custom-call.66
  365.9 11.7 cholesky.243
  378.2 9.8 custom-call.67
  393.5 11.7 cholesky.466
  406.0 9.8 custom-call.68
  420.4 11.7 cholesky.485
  432.9 9.8 custom-call.69
  447.0 12.1 cholesky.504
  459.9 9.8 custom-call.70
  474.1 11.7 cholesky.524
  486.6 9.8 custom-call.71
  500.3 11.7 cholesky.544
  512.8 9.8 custom-call.72
  525.7 11.7 cholesky.562
  547.8 4.8 select_select_fusion
  552.7 28.3 %while.1 = (s32[]{:T(128)}, f32[1024,1024]{0,1:T(8,128)}, s32[8,2]{0,1:T(2,128)S(1)}, f32[8,128,128]{2,1,0:T(8,128)}, s32[]{:T(128)}) while((s32[]{:T(128)}, f32[1024,1024]{0,1:T(8,128)}, s32[8,2]{0,1:T(2,128)S(1)}, f32[8,128,128]{2,1,0:T(8,128)}, s32[]{:T(128)}) %tuple.57), condition=%wide.while_cond, body=%wide.while_body.sunk | while | flops 2 | bytes 393829 | solution.py:36
  581.0 79.6 %custom-call.73 = f32[8,128,128]{1,2,0:T(8,128)S(1)} custom-call(f32[8,128,128]{2,1,0:T(8,128)} %get-tuple-element.9), custom_call_target="InvertDiagBlocksLowerTriangular" | custom-call | tf_op jit(solution)/shard_map/jit(_solve_triangular)/triangular_solve | solution.py:36
  685.0 55.8 %collective-permute-start = (bf16[1024,1024]{0,1:T(8,128)(2,1)S(1)}, bf16[1024,1024]{0,1:T(8,128)(2,1)}, u32[]{:S(2)}, u32[]{:S(2)}) collective-permute-start(bf16[1024,1024]{0,1:T(8,128)(2,1)S(1)} %bitcast.146), channel_id=1, source_target_pairs={{0,128},{128,0},{1,129},{129,1},{2,130},{130,2},{3,131},{131,3},{4... | collective-permute-start | bytes 6291464 | tf_op jit(solution)/shard_map/ppermute | solution.py:13
  744.8 5.0 fusion.50
  749.8 5.6 reshape.131
  755.5 257.7 %all-reduce.8.cloned.1.call-done = f32[256,4096]{1,0:T(8,128)} async-done(((f32[256,4096]{1,0:T(8,128)}), f32[256,4096]{1,0:T(8,128)}) %all-reduce.8.cloned.1.call-update) | async-done | bytes 4194320
  1014.7 118.7 %all-gather.3.cloned.1.call-done = bf16[256,1,4096]{2,1,0:T(2,128)(2,1)} async-done(((bf16[1,1,4096]{2,1,0:T(2,128)(2,1)}), bf16[256,1,4096]{2,1,0:T(2,128)(2,1)}) %all-gather.3.cloned.1.call-update) | async-done | bytes 2097168 | tf_op jit(solution)/shard_map/all_gather | solution.py:73
  1133.4 12.9 %reduce.50 = bf16[256,4096]{1,0:T(8,128)(2,1)S(1)} reduce(bf16[256,1,4096]{2,1,0:T(2,128)(2,1)} %all-gather.3.cloned.1.call-done, bf16[]{:T(256)} %constant.330), dimensions={1}, to_apply=%all-gather.reduce_sub_computation | reduce | bytes 4194306 | tf_op jit(solution)/shard_map/all_gather | solution.py:73
  1153.1 8.9 fusion.1
  1204.1 4.5 fusion.72
  1217.0 9.5 multiply_reduce_fusion
  (200 shorter events, 159.7 us)
Async XLA Ops:
  7.2 316.1 %all-reduce.6.cloned.1.call-start = ((), (), s32[]{:S(2)}) async-start(), calls=%async_computation | async-start | bytes 8388608 | tf_op jit(solution)/shard_map/psum | solution.py:50
  14.6 998.6 %all-reduce.8.cloned.1.call-start = ((), (), s32[]{:S(2)}) async-start(), calls=%async_computation.2 | async-start | bytes 8388608
  339.3 1.9 copy-start.3
  389.1 2.0 copy-start
  660.6 518.8 %copy-start.6 = (f32[8,128,128]{1,2,0:T(8,128)}, f32[8,128,128]{1,2,0:T(8,128)S(1)}, u32[]{:S(2)}) copy-start(f32[8,128,128]{1,2,0:T(8,128)S(1)} %custom-call.73) | copy-start | bytes 1572868
  660.6 4.5 copy-start.2
  685.0 64.8 %copy-start.5 = (bf16[1024,1024]{1,0:T(8,128)(2,1)}, bf16[1024,1024]{1,0:T(8,128)(2,1)S(1)}, u32[]{:S(2)}) copy-start(bf16[1024,1024]{1,0:T(8,128)(2,1)S(1)} %fusion.41) | copy-start | bytes 6291460
  685.0 59.8 %collective-permute-start = (bf16[1024,1024]{0,1:T(8,128)(2,1)S(1)}, bf16[1024,1024]{0,1:T(8,128)(2,1)}, u32[]{:S(2)}, u32[]{:S(2)}) collective-permute-start(bf16[1024,1024]{0,1:T(8,128)(2,1)S(1)} %bitcast.146), channel_id=1, source_target_pairs={{0,128},{128,0},{1,129},{129,1},{2,130},{130,2},{3,131},{131,3},{4... | collective-permute-start | bytes 6291464 | tf_op jit(solution)/shard_map/ppermute | solution.py:13
  755.4 378.0 %all-gather.3.cloned.1.call-start = ((), (), s32[]{:S(2)}) async-start(), calls=%async_computation.1 | async-start | bytes 4210688 | tf_op jit(solution)/shard_map/all_gather | solution.py:73
  1148.9 4.3 copy-start.4
  1204.1 10.6 copy-start.10
  1204.1 10.7 copy-start.9
  1204.1 10.8 copy-start.8
  1204.1 10.9 copy-start.7
  1213.5 3.5 copy-start.1
Sparse Core Ops, SparseCore 0:
  14.7 235.1 all-reduce.5
  755.5 257.5 all-reduce.7
  1017.5 115.9 all-gather.2
where the time goes:
time: 1240 us; the launch traced here: 1230 us
  waiting for transfers between devices  380 us (31%)
  blocking collectives  304 us (25%)
  other arithmetic  289 us (23%)
  matrix products  105 us (8%)
  local copies, waits for them, and re-layouts  78.2 us (6%)
  starting transfers between devices  56 us (5%)
  between operations  22.9 us (2%)
    psum x1, blocking collectives, on_device(): lax.psum((gram_part, column_part, count_part), ('depth', 'sub'))  304 us
    unnamed x4, waiting for transfers between devices  258 us
    another operation x30, other arithmetic, whitening(): factor_lower = jnp.linalg.cholesky(covariance)  168 us
    all_gather x1, waiting for transfers between devices, on_device(): lax.all_gather(share_bf, ('tower', 'depth', 'sub'), axis=0, tiled=True)  119 us
    another operation x3, other arithmetic, gradient_rows(): jax.scipy.linalg.solve_triangular(factor_lower, back_rows.T, lower=True,...  84.4 us
    ppermute x1, starting transfers between devices, from_partner(): return lax.ppermute(value, axis, pairs)  55.8 us
    another operation x15, matrix products, gradient_rows(): jax.scipy.linalg.solve_triangular(factor_lower, back_rows.T, lower=True,...  34.7 us
    another operation x40, local copies, waits for them, and re-layouts  28.2 us
  transfers between devices with their start and end apart: 4, of which 3 were waited for; matrix products, arithmetic and copies ran while one was open for 0% of the time, Pallas kernels for 0%

commit v1 on v0

v1 whole, which is shorter than its diff:
```python
import functools

import jax
import jax.numpy as jnp
from jax import lax
from jax.experimental import pallas as pl
from jax.experimental.pallas import tpu as pltpu
from jax.sharding import PartitionSpec as P

REG = 0.001
MESH = pl.DeviceIdType.MESH
F32, BF16 = jnp.float32, jnp.bfloat16
WIDTH = 1024
HALF = WIDTH // 2
TN = (((0,), (0,)), ((), ()))
NN = (((1,), (0,)), ((), ()))
NT = (((1,), (1,)), ((), ()))
SUB, YS, ZS = 4, 4, 8
BLOCK = 128


def moments_kernel(
    count_ref, x_ref, q_out, c_out, e_out, other_out,
    own, own_t, raw, q_src, c_src, first_in, first_sum, second_in, second_sum, third_in,
    e_x, e_y, e_z, sends, recvs, e_sends, e_recvs, pair_sends, pair_recvs,
):
    tower = lax.axis_index("tower")
    depth = lax.axis_index("depth")
    x = lax.axis_index("sub")
    y, z = depth // ZS, lax.rem(depth, ZS)
    rows = x_ref.shape[0]

    def at_x(p):
        return (tower, depth, p)

    def at_y(p):
        return (tower, p * ZS + z, x)

    def at_z(p):
        return (tower, y * ZS + p, x)

    partner = (1 - tower, depth, x)
    barrier = pltpu.get_barrier_semaphore()
    peers = [partner]
    peers += [at_x(lax.rem(x + d, SUB)) for d in range(1, SUB)]
    peers += [at_y(lax.rem(y + d, YS)) for d in range(1, YS)]
    peers += [at_z(lax.rem(z + d, ZS)) for d in range(1, ZS)]
    for peer in peers:
        pl.semaphore_signal(barrier, inc=1, device_id=peer, device_id_type=MESH)
    pl.semaphore_wait(barrier, len(peers))

    def remote(src, dst, send, recv, device):
        return pltpu.make_async_remote_copy(
            src_ref=src, dst_ref=dst, send_sem=send, recv_sem=recv, device_id=device, device_id_type=MESH
        )

    swap = remote(x_ref, raw, pair_sends.at[0], pair_recvs.at[0], partner)
    swap.start()

    count = count_ref[0]

    def mask_into(src, dst):
        def body(i, carry):
            part = pl.ds(pl.multiple_of(i * 128, 128), 128)
            row = lax.broadcasted_iota(jnp.int32, (128, WIDTH), 0) + i * 128
            dst[part, :] = jnp.where(row < count, src[part, :].astype(F32), 0.0).astype(BF16)
            return carry

        lax.fori_loop(0, rows // 128, body, 0)

    def dot(a, b):
        return jnp.dot(a, b, preferred_element_type=F32)

    mask_into(x_ref, own)

    def turn(i, carry):
        part = pl.ds(pl.multiple_of(i * 128, 128), 128)
        own_t[part, :] = own[:, part].T
        return carry

    lax.fori_loop(0, WIDTH // 128, turn, 0)
    upper = dot(own_t[:HALF, :], own[:, :HALF])
    lower = dot(own_t[HALF:, :], own[:, HALF:])
    r = lax.broadcasted_iota(jnp.int32, (HALF, HALF), 0)
    c = lax.broadcasted_iota(jnp.int32, (HALF, HALF), 1)
    q_src[:, :HALF] = jnp.where(r >= c, upper, lower)
    diagonal = jnp.sum(jnp.where(r == c, lower, 0.0), axis=0, keepdims=True)
    q_src[:, HALF:] = dot(own_t[HALF:, :], own[:, :HALF])

    streams = [(q_src, q_out, 0), (q_src, q_out, 1)]
    cross_out = c_out.at[tower]
    streams += [(c_src, cross_out, 0), (c_src, cross_out, 1)]

    def place(half):
        return ((x, at_x), (y, at_y)) if half == 0 else ((y, at_y), (x, at_x))

    def first(s):
        src, _, half = streams[s]
        (me, at), _ = place(half)
        copies = []
        for d in range(1, 4):
            to = lax.rem(me + d, 4)
            part = pl.ds(pl.multiple_of(half * 256 + to * 64, 64), 64)
            copies.append(remote(src.at[part, :], first_in.at[s, d - 1], sends.at[s, d - 1], recvs.at[s, d - 1], at(to)))
        return copies

    def second(s):
        _, _, half = streams[s]
        _, (me, at) = place(half)
        copies = []
        for d in range(1, 4):
            to = lax.rem(me + d, 4)
            part = pl.ds(pl.multiple_of(to * 16, 16), 16)
            copies.append(remote(first_sum.at[s, part, :], second_in.at[s, d - 1], sends.at[s, d + 2], recvs.at[s, d + 2], at(to)))
        return copies

    def third(s):
        copies = []
        for d in range(1, ZS):
            to = lax.rem(z + d, ZS)
            part = pl.ds(pl.multiple_of(to * 128, 128), 128)
            copies.append(remote(second_sum.at[s, :, part], third_in.at[s, d - 1], sends.at[s, d + 5], recvs.at[s, d + 5], at_z(to)))
        return copies

    def spot(s):
        _, out, half = streams[s]
        (p, _), (q, _) = place(half)
        return out, half * 256 + p * 64, half * 256 + p * 64 + q * 16

    def gather_third(s):
        out, _, row = spot(s)
        here = out.at[pl.ds(pl.multiple_of(row, 16), 16), pl.ds(pl.multiple_of(z * 128, 128), 128)]
        return [remote(here, here, sends.at[s, d + 12], recvs.at[s, d + 12], at_z(lax.rem(z + d, ZS))) for d in range(1, ZS)]

    def gather_second(s):
        out, _, row = spot(s)
        _, (me, at) = place(streams[s][2])
        here = out.at[pl.ds(pl.multiple_of(row, 16), 16), :]
        return [remote(here, here, sends.at[s, d + 19], recvs.at[s, d + 19], at(lax.rem(me + d, 4))) for d in range(1, 4)]

    def gather_first(s):
        out, row, _ = spot(s)
        (me, at), _ = place(streams[s][2])
        here = out.at[pl.ds(pl.multiple_of(row, 64), 64), :]
        return [remote(here, here, sends.at[s, d + 22], recvs.at[s, d + 22], at(lax.rem(me + d, 4))) for d in range(1, 4)]

    def start(copies):
        for copy in copies:
            copy.start()
        return copies

    def arrive(copies):
        for copy in copies:
            copy.wait()

    def sum_first(s):
        src, _, half = streams[s]
        (me, _), _ = place(half)
        part = pl.ds(pl.multiple_of(half * 256 + me * 64, 64), 64)
        first_sum[s] = (src[part, :] + first_in[s, 0]) + (first_in[s, 1] + first_in[s, 2])

    def sum_second(s):
        _, (me, _) = place(streams[s][2])
        part = pl.ds(pl.multiple_of(me * 16, 16), 16)
        second_sum[s] = (first_sum[s, part, :] + second_in[s, 0]) + (second_in[s, 1] + second_in[s, 2])

    def sum_third(s):
        out, _, row = spot(s)
        part = pl.ds(pl.multiple_of(z * 128, 128), 128)
        total = second_sum[s, :, part]
        for d in range(ZS - 1):
            total = total + third_in[s, d]
        out[pl.ds(pl.multiple_of(row, 16), 16), part] = total

    q_first = [start(first(s)) for s in (0, 1)]

    swap.wait()
    mask_into(raw, other_out)
    ones = jnp.ones((8, rows), BF16)
    own_sum = dot(ones, own[...])[:1]
    other_sum = dot(ones, other_out[...])[:1]
    is_log = tower == 0
    e_x[x] = jnp.concatenate(
        [
            jnp.where(is_log, own_sum, other_sum),
            jnp.where(is_log, other_sum, own_sum),
            jnp.concatenate([diagonal, diagonal], axis=1),
            jnp.full((5, WIDTH), count, jnp.int32).astype(F32),
        ],
        axis=0,
    )
    e_copies = start(
        [remote(e_x.at[x], e_x.at[x], e_sends.at[d - 1], e_recvs.at[d - 1], at_x(lax.rem(x + d, SUB))) for d in range(1, SUB)]
    )

    @pl.when(is_log)
    def _():
        c_src[...] = dot(own_t[:HALF, :], other_out[...])

    @pl.when(tower == 1)
    def _():
        c_src[...] = lax.dot_general(other_out[:, HALF:], own[...], TN, preferred_element_type=F32)

    c_first = [start(first(s)) for s in (2, 3)]

    arrive(e_copies)
    e_y[y] = (e_x[0] + e_x[1]) + (e_x[2] + e_x[3])
    e_copies = start(
        [remote(e_y.at[y], e_y.at[y], e_sends.at[d + 2], e_recvs.at[d + 2], at_y(lax.rem(y + d, YS))) for d in range(1, YS)]
    )
    moving = {}
    for s, copies in zip((0, 1), q_first):
        arrive(copies)
        sum_first(s)
        moving[s] = start(second(s))
    arrive(e_copies)
    e_z[z] = (e_y[0] + e_y[1]) + (e_y[2] + e_y[3])
    e_copies = start(
        [remote(e_z.at[z], e_z.at[z], e_sends.at[d + 5], e_recvs.at[d + 5], at_z(lax.rem(z + d, ZS))) for d in range(1, ZS)]
    )
    for s in (0, 1):
        arrive(moving[s])
        sum_second(s)
        moving[s] = start(third(s))
    for s in (0, 1):
        arrive(moving[s])
        sum_third(s)
        moving[s] = start(gather_third(s))
    for s, copies in zip((2, 3), c_first):
        arrive(copies)
        sum_first(s)
        moving[s] = start(second(s))
    for s in (0, 1):
        arrive(moving[s])
        moving[s] = start(gather_second(s))
    for s in (2, 3):
        arrive(moving[s])
        sum_second(s)
        moving[s] = start(third(s))
    for s in (0, 1):
        arrive(moving[s])
        moving[s] = start(gather_first(s))
    for s in (2, 3):
        arrive(moving[s])
        sum_third(s)
        moving[s] = start(gather_third(s))
    for s in (2, 3):
        arrive(moving[s])
        moving[s] = start(gather_second(s))
    for s in (2, 3):
        arrive(moving[s])
        moving[s] = start(gather_first(s))
    arrive(e_copies)
    total = e_z[0]
    for d in range(1, ZS):
        total = total + e_z[d]
    e_out[...] = total
    for s in (0, 1):
        arrive(moving[s])
    for s in (2, 3):
        arrive(moving[s])
    across = remote(cross_out, cross_out, pair_sends.at[1], pair_recvs.at[1], partner)
    across.start()
    across.wait()


def moments(block_rows, counts):
    vmem = pl.BlockSpec(memory_space=pltpu.VMEM)
    rows = block_rows.shape[0]
    dma = pltpu.SemaphoreType.DMA
    return pl.pallas_call(
        moments_kernel,
        out_shape=(
            jax.ShapeDtypeStruct((HALF, WIDTH), F32),
            jax.ShapeDtypeStruct((2, HALF, WIDTH), F32),
            jax.ShapeDtypeStruct((8, WIDTH), F32),
            jax.ShapeDtypeStruct((rows, WIDTH), BF16),
        ),
        in_specs=[pl.BlockSpec(memory_space=pltpu.SMEM), vmem],
        out_specs=(vmem,) * 4,
        scratch_shapes=[
            pltpu.VMEM((rows, WIDTH), BF16),
            pltpu.VMEM((WIDTH, rows), BF16),
            pltpu.VMEM((rows, WIDTH), BF16),
            pltpu.VMEM((HALF, WIDTH), F32),
            pltpu.VMEM((HALF, WIDTH), F32),
            pltpu.VMEM((4, 3, 64, WIDTH), F32),
            pltpu.VMEM((4, 64, WIDTH), F32),
            pltpu.VMEM((4, 3, 16, WIDTH), F32),
            pltpu.VMEM((4, 16, WIDTH), F32),
            pltpu.VMEM((4, 7, 16, 128), F32),
            pltpu.VMEM((SUB, 8, WIDTH), F32),
            pltpu.VMEM((YS, 8, WIDTH), F32),
            pltpu.VMEM((ZS, 8, WIDTH), F32),
            dma((4, 26)),
            dma((4, 26)),
            dma((13,)),
            dma((13,)),
            dma((2,)),
            dma((2,)),
        ],
        compiler_params=pltpu.CompilerParams(collective_id=0, has_side_effects=True, vmem_limit_bytes=48 * 2**20),
        name="moments",
    )(counts, block_rows)


def split(value):
    high = value.astype(BF16)
    return high, (value - high.astype(F32)).astype(BF16)


def dot_parts(left, right, dims):
    (lh, ll), (rh, rl) = left, right
    dot = functools.partial(lax.dot_general, dimension_numbers=dims, preferred_element_type=F32)
    return dot(lh, rh) + (dot(lh, rl) + dot(ll, rh))


def dot_wide(left, right, dims=NN):
    return dot_parts(split(left), split(right), dims)


def inverse_block(block):
    width = block.shape[1]
    rows = lax.broadcasted_iota(jnp.int32, (8, width), 0)
    lanes = lax.broadcasted_iota(jnp.int32, (8, width), 1)

    def spread(value):
        return jnp.broadcast_to(value, (8, width))

    def key(i, j):
        return (i, j) if i <= j else (j, i)

    groups = [block[8 * i : 8 * i + 8] for i in range(width // 8)]
    for g, panel in enumerate(groups):
        panel = groups[g]
        first = 8 * g
        columns = [spread(panel[:, first + j : first + j + 1]) for j in range(8)]
        pivot = {(i, j): spread(columns[j][i : i + 1, :]) for j in range(8) for i in range(j + 1)}
        for k in range(8):
            inverse = 1.0 / pivot[k, k]
            old = {i: pivot[key(i, k)] for i in range(8) if i != k}
            scaled = {i: old[i] * inverse for i in old}
            for j in range(8):
                for i in range(j + 1):
                    if i != k and j != k:
                        pivot[i, j] = pivot[i, j] - scaled[i] * old[j]
            for i in old:
                pivot[key(i, k)] = scaled[i]
            pivot[k, k] = -inverse
        turned = []
        for j in range(8):
            column = pivot[key(7, j)]
            for i in range(6, -1, -1):
                column = jnp.where(rows == i, pivot[key(i, j)], column)
            turned.append(-column)
        solved = turned[0] * spread(panel[:1, :])
        for j in range(1, 8):
            solved = solved + turned[j] * spread(panel[j : j + 1, :])
        for j in range(8):
            solved = jnp.where(lanes == first + j, turned[j], solved)
        lines = [spread(solved[j : j + 1, :]) for j in range(8)]
        inside = (lanes >= first) & (lanes < first + 8)
        for i in [*range(g + 1, width // 8), *range(g)]:
            terms = [groups[i][:, first + j : first + j + 1] * lines[j] for j in range(8)]
            even = (terms[0] + terms[2]) + (terms[4] + terms[6])
            odd = (terms[1] + terms[3]) + (terms[5] + terms[7])
            groups[i] = jnp.where(inside, 0.0, groups[i]) - (even + odd)
        groups[g] = solved
    return jnp.concatenate(groups, axis=0)


def as_column(row):
    return jnp.broadcast_to(row, (8, row.shape[1])).T[:, :1]


def inverse_kernel(q_ref, e_ref, a_ref):
    tower = lax.axis_index("tower")
    total = e_ref[3:4, :1]
    sums = e_ref[pl.ds(tower, 1), :]
    column = as_column(sums)
    mean = sums / total
    r = lax.broadcasted_iota(jnp.int32, (HALF, HALF), 0)
    c = lax.broadcasted_iota(jnp.int32, (HALF, HALF), 1)
    eye = jnp.where(r == c, REG, 0.0)

    def covariance(gram, i, j):
        outer = column[i * HALF : (i + 1) * HALF] * mean[:, j * HALF : (j + 1) * HALF]
        value = (gram - outer) / (total - 1.0)
        a_ref[i * HALF : (i + 1) * HALF, j * HALF : (j + 1) * HALF] = value + eye if i == j else value

    shared = q_ref[:, :HALF]
    turned = shared.T
    covariance(jnp.where(r >= c, shared, turned), 0, 0)
    covariance(jnp.where(r == c, e_ref[2:3, :HALF], jnp.where(r > c, turned, shared)), 1, 1)
    covariance(q_ref[:, HALF:], 1, 0)
    covariance(q_ref[:, HALF:].T, 0, 1)

    def step(k, carry):
        here = pl.ds(pl.multiple_of(k * BLOCK, BLOCK), BLOCK)
        inverse = inverse_block(a_ref[here, here])
        side = a_ref[:, here]
        solved = dot_wide(inverse, a_ref[here, :])
        for part in range(4):
            columns = slice(part * 256, (part + 1) * 256)
            a_ref[:, columns] = a_ref[:, columns] - dot_wide(side, solved[:, columns])
        a_ref[:, here] = -dot_wide(side, inverse)
        a_ref[here, :] = solved
        a_ref[here, here] = inverse
        return carry

    lax.fori_loop(0, WIDTH // BLOCK, step, 0)


def cross_covariance(c_ref, e_ref, column, rows, columns):
    total = e_ref[3:4, :1]
    mean = e_ref[1:2, :] / total
    return (c_ref[rows, columns] - column[rows] * mean[:, columns]) / (total - 1.0)


CHUNKS = [slice(i * 256, (i + 1) * 256) for i in range(WIDTH // 256)]
ALL = slice(None)


def residual_kernel(count_ref, a_ref, c_ref, e_ref, own_ref, other_ref, p_high, p_low, r_ref, a_high, a_low):
    tower = lax.axis_index("tower")
    total = e_ref[3:4, :1]
    own_mean = e_ref[pl.ds(tower, 1), :] / total
    other_mean = e_ref[pl.ds(1 - tower, 1), :] / total
    column = as_column(e_ref[0:1, :])
    high, low = split(a_ref[...])
    a_high[...] = high
    a_low[...] = low

    for part in CHUNKS:

        @pl.when(tower == 0)
        def _():
            cross = split(cross_covariance(c_ref, e_ref, column, ALL, part))
            ph, plow = split(dot_parts((a_high[...], a_low[...]), cross, NN))
            p_high[:, part] = ph
            p_low[:, part] = plow

        @pl.when(tower == 1)
        def _():
            cross = split(cross_covariance(c_ref, e_ref, column, part, ALL))
            ph, plow = split(dot_parts((a_high[...], a_low[...]), cross, NT))
            p_high[:, part] = ph
            p_low[:, part] = plow

    rows = own_ref.shape[0]
    valid = lax.broadcasted_iota(jnp.int32, (rows, 256), 0) < count_ref[0]
    for part in CHUNKS:
        ph, plow = p_high[:, part], p_low[:, part]
        shift = dot_parts(split(jnp.broadcast_to(own_mean, (8, WIDTH))), (ph, plow), NN)[:1]
        fitted = jnp.dot(own_ref[...], ph, preferred_element_type=F32) + jnp.dot(
            own_ref[...], plow, preferred_element_type=F32
        )
        left = (other_ref[:, part].astype(F32) - fitted) - (other_mean[:, part] - shift)
        r_ref[:, part] = jnp.where(valid, left, 0.0).astype(BF16)


def back_kernel(a_ref, p_high, p_low, c_ref, e_ref, m_high, m_low, corr_ref, a_high, a_low):
    column = as_column(e_ref[0:1, :])
    high, low = split(a_ref[...])
    a_high[...] = high
    a_low[...] = low
    corr = jnp.zeros((1, 256), F32)
    for part in CHUNKS:
        back = dot_parts((a_high[...], a_low[...]), (p_high[part, :], p_low[part, :]), NT)
        mh, ml = split(back)
        m_high[:, part] = mh
        m_low[:, part] = ml
        cross = cross_covariance(c_ref, e_ref, column, ALL, part)
        corr = corr + jnp.sum(back * cross, axis=0, keepdims=True)
    corr_ref[...] = jnp.broadcast_to(jnp.sum(corr, axis=1, keepdims=True) / WIDTH, (8, 128))


def gradient_kernel(r_ref, m_high, m_low, out_ref):
    for part in CHUNKS:
        value = jnp.dot(r_ref[...], m_high[:, part], preferred_element_type=F32) + jnp.dot(
            r_ref[...], m_low[:, part], preferred_element_type=F32
        )
        out_ref[:, part] = value.astype(BF16)


VMEM = pl.BlockSpec(memory_space=pltpu.VMEM)
SMEM = pl.BlockSpec(memory_space=pltpu.SMEM)


def local_call(kernel, name, shapes, args, passes, scratch=()):
    specs = [SMEM if arg.dtype == jnp.int32 else VMEM for arg in args]
    return pl.pallas_call(
        kernel,
        out_shape=[jax.ShapeDtypeStruct(shape, dtype) for shape, dtype in shapes],
        in_specs=specs,
        out_specs=[VMEM] * len(shapes),
        scratch_shapes=scratch,
        compiler_params=pltpu.CompilerParams(vmem_limit_bytes=56 * 2**20),
        cost_estimate=pl.CostEstimate(
            flops=passes * 2 * WIDTH**3, bytes_accessed=16 * 2**20, transcendentals=0
        ),
        name=name,
    )(*args)


def on_device(embeds, counts):
    square = (WIDTH, WIDTH)
    block_rows = embeds[0]
    gram, cross, sums, other_rows = moments(block_rows, counts)
    cross = cross.reshape(square)
    (inverse,) = local_call(inverse_kernel, "inverse", [(square, F32)], (gram, sums), 30)
    pairs = [(0, 1), (1, 0)]
    other_inverse = lax.ppermute(inverse, "tower", pairs)
    halves = [pltpu.VMEM(square, BF16)] * 2
    p_high, p_low, residual = local_call(
        residual_kernel,
        "residual",
        [(square, BF16), (square, BF16), (block_rows.shape, BF16)],
        (counts, inverse, cross, sums, block_rows, other_rows),
        5,
        halves,
    )
    m_high, m_low, corr = local_call(
        back_kernel,
        "back",
        [(square, BF16), (square, BF16), ((8, 128), F32)],
        (other_inverse, p_high, p_low, cross, sums),
        3,
        halves,
    )
    log_corr = lax.ppermute(corr, "tower", pairs)
    (gradient,) = local_call(gradient_kernel, "gradient", [(block_rows.shape, BF16)], (residual, m_high, m_low), 2)
    corr_mean = jnp.where(lax.axis_index("tower") == 1, corr, log_corr)[0, 0]
    return gradient[None], corr_mean


def solution(mesh):
    placed = (P("tower", ("depth", "sub"), None), P(("depth", "sub")))
    return jax.shard_map(
        on_device,
        mesh=mesh,
        in_specs=placed,
        out_specs=(P("tower", ("depth", "sub"), None), P()),
        check_vma=False,
    )
```

time: 1240 us -> 223 us (0.18)
  waiting for transfers between devices: 380 us -> 0.01 us
  blocking collectives: 304 us -> 0 us
  other arithmetic: 289 us -> 0.01 us
  Pallas kernels: 0 us -> 213 us
  matrix products: 105 us -> 0 us
  local copies, waits for them, and re-layouts: 78.2 us -> 3.78 us
  starting transfers between devices: 56 us -> 0.73 us
  between operations: 22.9 us -> 1.57 us
    psum x1 -> x0, blocking collectives: 304 us -> none  [on_device(): lax.psum((gram_part, column_part, count_part), ('depth', 'sub'))]
    unnamed x4 -> x0, waiting for transfers between devices: 258 us -> none
    another operation x33 -> x0, other arithmetic: 252 us -> none  [the longest x30 168 us: whitening(): factor_lower = jnp.linalg.cholesky(covariance)]
    pallas_call x0 -> x5, Pallas kernels: none -> 213 us  [the longest x4 115 us: local_call(): pl.pallas_call(kernel, out_shape=[jax.ShapeDtypeStruct(shape, dtype) for...]
    all_gather x1 -> x0, waiting for transfers between devices: 119 us -> none  [on_device(): lax.all_gather(share_bf, ('tower', 'depth', 'sub'), axis=0, tiled=True)]
    another operation x44 -> x0, matrix products: 84 us -> none  [the longest x15 34.7 us: gradient_rows(): jax.scipy.linalg.solve_triangular(factor_lower, back_rows.T, lower=True,...]
    ppermute x1 -> x2, starting transfers between devices: 55.8 us -> 0.73 us  [the longest x1 0.59 us: on_device(): log_corr = lax.ppermute(corr, 'tower', pairs)]
    another operation x78 -> x0, local copies, waits for them, and re-layouts: 41.8 us -> none
  transfers between devices with their start and end apart: 4 -> 2, of which waited for: 3 -> 0; matrix products, arithmetic and copies ran while one was open for 0% -> 0% of each run, Pallas kernels for 0% -> 13%
where the time goes in v1:
time: 223 us; the launch traced here: 219 us
  Pallas kernels  213 us (96%)
  local copies, waits for them, and re-layouts  3.78 us (2%)
    pallas_call x4, Pallas kernels, local_call(): pl.pallas_call(kernel, out_shape=[jax.ShapeDtypeStruct(shape, dtype) for...  115 us
    pallas_call x1, Pallas kernels, moments(): pl.pallas_call(moments_kernel, out_shape=(jax.ShapeDtypeStruct((HALF, WID...  98.7 us
  transfers between devices with their start and end apart: 2, of which 0 were waited for; matrix products, arithmetic and copies ran while one was open for 0% of the time, Pallas kernels for 13%

profile of v1, /device:TPU:1, one launch (start us, length us, event | category | flops | bytes accessed | tf_op | source)
XLA Modules:
  0.0 219.4 jit_solution(4177771275063169071)
XLA Ops:
  1.3 98.7 %moments.1 = (f32[512,1024]{1,0:T(8,128)S(1)}, f32[2,512,1024]{2,1,0:T(8,128)}, f32[8,1024]{1,0:T(8,128)S(1)}, bf16[1024,1024]{1,0:T(8,128)(2,1)S(1)}) custom-call(s32[1]{0:T(128)S(6)} %copy.4.count_ref, bf16[1024,1024]{1,0:T(8,128)(2,1)} %bitcast.4), custom_call_target="tpu_custom_call" | custom-call | tf_op jit(solution)/shard_map/moments/pallas_call | solution.py:271
  100.0 0.0 copy-start
  100.0 1.3 copy-done
  101.4 0.0 copy-start.1
  101.4 1.3 copy-done.1
  102.7 0.0 copy-start.2
  102.7 0.6 copy-done.2
  103.3 71.4 %inverse.1.a_ref = f32[1024,1024]{1,0:T(8,128)} custom-call(f32[512,1024]{1,0:T(8,128)} %copy-done.1, f32[8,1024]{1,0:T(8,128)} %copy-done.2), custom_call_target="tpu_custom_call" | custom-call | flops 64424509440 | bytes 16777216 | tf_op jit(solution)/shard_map/inverse/pallas_call | solution.py:492
  174.7 0.1 collective-permute-start
  174.8 20.8 %residual.1 = (bf16[1024,1024]{1,0:T(8,128)(2,1)}, bf16[1024,1024]{1,0:T(8,128)(2,1)}, bf16[1024,1024]{1,0:T(8,128)(2,1)}) custom-call(s32[1]{0:T(128)S(6)} %copy.4.count_ref, f32[1024,1024]{1,0:T(8,128)} %inverse.1.a_ref, f32[1024,1024]{1,0:T(8,128)} %bitcast.6, f32[8,1024]{1,0:T(8,128)} %copy-done.2, bf16[1024,1024]{1,0:T(8,128)(2,1)} %bitcast.5, ...), custom_call_target="tpu_custom_call" | custom-call | flops 10737418240 | bytes 16777216 | tf_op jit(solution)/shard_map/residual/pallas_call | solution.py:492
  195.6 0.0 collective-permute-done.a_ref
  195.6 13.8 %back.1 = (bf16[1024,1024]{1,0:T(8,128)(2,1)}, bf16[1024,1024]{1,0:T(8,128)(2,1)}, f32[8,128]{1,0:T(8,128)}) custom-call(f32[1024,1024]{1,0:T(8,128)} %collective-permute-done.a_ref, bf16[1024,1024]{1,0:T(8,128)(2,1)} %get-tuple-element.17.p_high, bf16[1024,1024]{1,0:T(8,128)(2,1)} %get-tuple-element.18.p_low, f32[1024,1024]{1,0:T(8,128)} %bitcast.7, ...), custom_call_target="tpu_custom_call" | custom-call | flops 6442450944 | bytes 16777216 | tf_op jit(solution)/shard_map/back/pallas_call | solution.py:492
  209.4 0.6 collective-permute-start.1
  210.0 0.0 copy-start.3
  210.0 8.7 %gradient.1 = bf16[1024,1024]{1,0:T(8,128)(2,1)} custom-call(bf16[1024,1024]{1,0:T(8,128)(2,1)} %get-tuple-element.16.r_ref, bf16[1024,1024]{1,0:T(8,128)(2,1)} %get-tuple-element.19.m_high, bf16[1024,1024]{1,0:T(8,128)(2,1)} %get-tuple-element.20.m_low), custom_call_target="tpu_custom_call" | custom-call | flops 4294967296 | bytes 16777216 | tf_op jit(solution)/shard_map/gradient/pallas_call | solution.py:492
  218.7 0.0 collective-permute-done.1
  218.7 0.0 copy-done.3
  218.7 0.5 slice.3
  (1 shorter events, 0.0 us)
Async XLA Ops:
  100.0 1.3 copy-start
  101.4 1.3 copy-start.1
  102.7 0.6 copy-start.2
  174.7 20.9 %collective-permute-start = (f32[1024,1024]{1,0:T(8,128)}, f32[1024,1024]{1,0:T(8,128)}, u32[]{:S(2)}, u32[]{:S(2)}) collective-permute-start(f32[1024,1024]{1,0:T(8,128)} %inverse.1.a_ref), channel_id=1, source_target_pairs={{0,128},{128,0},{1,129},{129,1},{2,130},{130,2},{3,131},{131,3},{4... | collective-permute-start | bytes 12582920 | tf_op jit(solution)/shard_map/ppermute | solution.py:513
  209.4 9.3 %collective-permute-start.1 = (f32[8,128]{1,0:T(8,128)}, f32[8,128]{1,0:T(8,128)S(1)}, u32[]{:S(2)}, u32[]{:S(2)}) collective-permute-start(f32[8,128]{1,0:T(8,128)} %get-tuple-element.21), channel_id=1, source_target_pairs={{0,128},{128,0},{1,129},{129,1},{2,130},{130,2},{3,131},{131,3},{4... | collective-permute-start | bytes 12296 | tf_op jit(solution)/shard_map/ppermute | solution.py:531
  210.0 8.7 %copy-start.3 = (f32[8,128]{1,0:T(8,128)S(1)}, f32[8,128]{1,0:T(8,128)}, u32[]{:S(2)}) copy-start(f32[8,128]{1,0:T(8,128)} %get-tuple-element.21) | copy-start | bytes 12292
